TPU v7x, 128 devices: a whole 4x4x4 slice. The times are simulated.
128 devices in a mesh: fam: 4 (over z), ctx: 32 (over x, y, core).
Axes of the slice: x: 4, y: 4, z: 4, core: 2. Of those that a mesh axis runs over, the one named last changes fastest.
Arguments:
- queries: bfloat16 [4, 16384, 1024], P('fam', 'ctx'), may hold values from -7 to 7
- key_rows: bfloat16 [4, 16384, 1024], P('fam', 'ctx'), may hold values from -4 to 4
- value_rows: bfloat16 [4, 16384, 1024], P('fam', 'ctx'), may hold values from -6 to 6
- cotangent: bfloat16 [4, 16384, 1024], P('fam', 'ctx'), may hold values from -6 to 6
- out_weight: bfloat16 [1024, 1024], replicated, may hold values from -0.1875 to 0.1875
- prot_blocks: int32 [4, 32], P('fam'), may hold values from 1 to 8, 128 in all within a row
- last_fill: int32 [4, 32], P('fam'), may hold values from 1 to 128
- memory_slots: int32 [4, 512], P('fam'), may hold values from 0 to 511
Outputs:
- query_grad: bfloat16 [4, 16384, 1024], P('fam', 'ctx')
- key_grad: bfloat16 [4, 16384, 1024], P('fam', 'ctx')
- value_grad: bfloat16 [4, 16384, 1024], P('fam', 'ctx')
- weight_grad: float32 [1024, 1024], replicated
Inputs may be any that keep to these rules, and one draw needn't show every extreme that they name: `prot_blocks`: each family's protein lengths, in blocks, sum to 128, and the longest has exactly 8 blocks.
All inputs are finite; a program needn't handle non-finite values.
Results may differ from a plain program's by a relative error of at most 0.015.
Values may be sent and summed in bfloat16 or wider, within the bound.
A program may use at most 128 MiB of HBM per device.

v0:
```python
import jax
import jax.numpy as jnp
from jax import lax
from jax.sharding import PartitionSpec as P

HEAD_DIM = 64
W = 512
BLK = 128
NEG_FILL = -1e30


def passed_along(value, axis, steps):
    count = lax.axis_size(axis)
    initial, last = (max(0, -steps), min(count, count - steps))
    return lax.ppermute(value, axis, [(source, source + steps) for source in range(initial, last)])


def protein_tables(prot_blocks, last_fill):
    prot_ends = jnp.cumsum(prot_blocks)
    starts = prot_ends - prot_blocks
    valid_len = (prot_blocks - 1) * BLK + last_fill
    return (prot_ends, starts, valid_len)


def token_info(positions, tables):
    prot_ends, starts, valid_len = tables
    prot_count = prot_ends.shape[0]
    block_ids = jnp.floor_divide(positions, BLK)
    protein = jnp.sum((block_ids[:, None] >= prot_ends[None, :]).astype(jnp.int32), axis=1)
    onehot = protein[:, None] == jnp.arange(prot_count, dtype=jnp.int32)[None, :]
    first_block = jnp.sum(jnp.where(onehot, starts[None, :], 0), axis=1)
    allowed = jnp.sum(jnp.where(onehot, valid_len[None, :], 0), axis=1)
    is_valid = (positions >= 0) & (protein < prot_count) & (positions - first_block * BLK < allowed)
    return (protein, is_valid)


def band_mask(query_pos, query_info, key_pos, key_info):
    return (
        query_info[1][:, None]
        & key_info[1][None, :]
        & (query_info[0][:, None] == key_info[0][None, :])
        & (key_pos[None, :] <= query_pos[:, None])
        & (query_pos[:, None] - key_pos[None, :] < W)
    )


def columns_of(array, column, span):
    return lax.dynamic_slice_in_dim(array, column, span, 1)


def add_into(target, update, row_start, column):
    row_index = jnp.asarray(row_start, jnp.int32)
    current = lax.dynamic_slice(target, (row_index, column), update.shape)
    return lax.dynamic_update_slice(target, current + update, (row_index, column))


def attend(query_blk, grad_blk, key_blk, value_blk, live_mask):
    scale = HEAD_DIM ** (-0.5)
    scores = (
        jnp.einsum("qge,kge->gqk", query_blk, key_blk, preferred_element_type=jnp.float32) * scale
    )
    live = live_mask[None]
    shifted = jnp.where(live, scores, NEG_FILL)
    row_max = jnp.max(shifted, axis=-1, keepdims=True)
    expo = jnp.where(live, jnp.exp(shifted - row_max), 0.0)
    row_sum = jnp.maximum(jnp.sum(expo, axis=-1, keepdims=True), 1.0)
    attn_prob = expo / row_sum
    prob_half = attn_prob.astype(jnp.bfloat16)
    attended = jnp.einsum(
        "gqk,kge->qge", prob_half, value_blk, preferred_element_type=jnp.float32
    ).astype(jnp.bfloat16)
    grad_prob = jnp.einsum("qge,kge->gqk", grad_blk, value_blk, preferred_element_type=jnp.float32)
    row_dot = jnp.sum(attn_prob * grad_prob, axis=-1, keepdims=True)
    grad_score = (attn_prob * (grad_prob - row_dot) * scale).astype(jnp.bfloat16)
    grad_query = jnp.einsum("gqk,kge->qge", grad_score, key_blk, preferred_element_type=jnp.float32)
    grad_key = jnp.einsum("gqk,qge->kge", grad_score, query_blk, preferred_element_type=jnp.float32)
    grad_value = jnp.einsum("gqk,qge->kge", prob_half, grad_blk, preferred_element_type=jnp.float32)
    return (attended, grad_query, grad_key, grad_value, row_max, row_sum, row_dot)


def per_device(
    queries, key_rows, value_rows, cotangent, out_weight, prot_blocks, last_fill, memory_slots
):
    query_loc = queries[0]
    key_loc = key_rows[0]
    value_loc = value_rows[0]
    grad_out = cotangent[0]
    tables = protein_tables(prot_blocks[0], last_fill[0])
    slots = memory_slots[0]
    tokens, width = query_loc.shape
    span = 2 * HEAD_DIM
    pair_count = width // span
    heads_total = width // HEAD_DIM
    ctx_size = lax.axis_size("ctx")
    ctx_index = lax.axis_index("ctx")
    slot_total = slots.shape[0]
    slot_dev = slot_total // ctx_size
    base = ctx_index * tokens
    positions = base + jnp.arange(tokens, dtype=jnp.int32)
    own_info = token_info(positions, tables)
    ext_pos = base - W + jnp.arange(W + tokens, dtype=jnp.int32)
    ext_info = token_info(ext_pos, tables)
    source = jnp.arange(slot_total, dtype=jnp.int32) // slot_dev * tokens + slots
    mem_info = token_info(source, tables)
    own_slots = lax.dynamic_slice_in_dim(slots, ctx_index * slot_dev, slot_dev)
    mem_keys, mem_values = (
        lax.all_gather(key_loc[own_slots], "ctx", axis=0, tiled=True),
        lax.all_gather(value_loc[own_slots], "ctx", axis=0, tiled=True),
    )
    halo_keys, halo_values = passed_along((key_loc, value_loc), "ctx", 1)
    ext_keys = jnp.concatenate([halo_keys, key_loc], axis=0)
    ext_values = jnp.concatenate([halo_values, value_loc], axis=0)
    grad_attn = jnp.einsum(
        "te,de->td", grad_out, out_weight, preferred_element_type=jnp.float32
    ).astype(jnp.bfloat16)
    masks = []
    query_info = (own_info[0], own_info[1])
    key_info = (ext_info[0], ext_info[1])
    band = band_mask(positions, query_info, ext_pos, key_info)
    memory = (
        query_info[1][:, None]
        & mem_info[1][None, :]
        & (mem_info[0][None, :] < query_info[0][:, None])
    )
    masks.append(jnp.concatenate([band, memory], axis=1))

    def pair_step(head_pair, carry):
        (
            query_grad,
            band_kgrad,
            band_vgrad,
            mem_kgrad,
            mem_vgrad,
            attn_rows,
            stat_max,
            stat_sum,
            stat_dot,
        ) = carry
        column = head_pair * span
        query_pair = columns_of(query_loc, column, span).reshape(tokens, 2, HEAD_DIM)
        dout_pair = columns_of(grad_attn, column, span).reshape(tokens, 2, HEAD_DIM)
        key_band = columns_of(ext_keys, column, span).reshape(W + tokens, 2, HEAD_DIM)
        value_band = columns_of(ext_values, column, span).reshape(W + tokens, 2, HEAD_DIM)
        key_memory = columns_of(mem_keys, column, span).reshape(slot_total, 2, HEAD_DIM)
        value_memory = columns_of(mem_values, column, span).reshape(slot_total, 2, HEAD_DIM)
        key_blk = jnp.concatenate([key_band, key_memory], axis=0)
        value_blk = jnp.concatenate([value_band, value_memory], axis=0)
        attended, grad_query, grad_key, grad_value, row_max, row_sum, row_dot = attend(
            query_pair, dout_pair, key_blk, value_blk, masks[0]
        )
        row_index = jnp.asarray(0, jnp.int32)
        query_grad = lax.dynamic_update_slice(
            query_grad, grad_query.reshape(W, span), (row_index, column)
        )
        attn_rows = lax.dynamic_update_slice(
            attn_rows, attended.reshape(W, span), (row_index, column)
        )
        band_kgrad = add_into(band_kgrad, grad_key[: 2 * W].reshape(2 * W, span), 0, column)
        band_vgrad = add_into(band_vgrad, grad_value[: 2 * W].reshape(2 * W, span), 0, column)
        mem_kgrad = add_into(mem_kgrad, grad_key[2 * W :].reshape(slot_total, span), 0, column)
        mem_vgrad = add_into(mem_vgrad, grad_value[2 * W :].reshape(slot_total, span), 0, column)
        stat_col = head_pair * 2
        zero_row = jnp.asarray(0, jnp.int32)
        stat_max = lax.dynamic_update_slice(stat_max, row_max[:, :, 0].T, (zero_row, stat_col))
        stat_sum = lax.dynamic_update_slice(stat_sum, row_sum[:, :, 0].T, (zero_row, stat_col))
        stat_dot = lax.dynamic_update_slice(stat_dot, row_dot[:, :, 0].T, (zero_row, stat_col))
        return (
            query_grad,
            band_kgrad,
            band_vgrad,
            mem_kgrad,
            mem_vgrad,
            attn_rows,
            stat_max,
            stat_sum,
            stat_dot,
        )

    init = (
        jnp.zeros((tokens, width), jnp.float32),
        jnp.zeros((W + tokens, width), jnp.float32),
        jnp.zeros((W + tokens, width), jnp.float32),
        jnp.zeros((slot_total, width), jnp.float32),
        jnp.zeros((slot_total, width), jnp.float32),
        jnp.zeros((tokens, width), jnp.bfloat16),
        jnp.zeros((W, heads_total), jnp.float32),
        jnp.zeros((W, heads_total), jnp.float32),
        jnp.zeros((W, heads_total), jnp.float32),
    )
    (
        query_grad,
        band_kgrad,
        band_vgrad,
        mem_kgrad,
        mem_vgrad,
        attn_rows,
        stat_max,
        stat_sum,
        stat_dot,
    ) = lax.fori_loop(0, pair_count, pair_step, init)
    own_kgrad = band_kgrad[W:]
    own_vgrad = band_vgrad[W:]
    back_kgrad, back_vgrad = (
        passed_along(band_kgrad[:W].astype(jnp.bfloat16), "ctx", -1).astype(jnp.float32),
        passed_along(band_vgrad[:W].astype(jnp.bfloat16), "ctx", -1).astype(jnp.float32),
    )
    own_kgrad = own_kgrad.at[tokens - W :].add(back_kgrad)
    own_vgrad = own_vgrad.at[tokens - W :].add(back_vgrad)
    got_kgrad, got_vgrad = (
        lax.psum_scatter(
            mem_kgrad.astype(jnp.bfloat16), "ctx", scatter_dimension=0, tiled=True
        ).astype(jnp.float32),
        lax.psum_scatter(
            mem_vgrad.astype(jnp.bfloat16), "ctx", scatter_dimension=0, tiled=True
        ).astype(jnp.float32),
    )
    own_kgrad = own_kgrad.at[own_slots].add(got_kgrad)
    own_vgrad = own_vgrad.at[own_slots].add(got_vgrad)
    weight_part = lax.dot_general(
        attn_rows, grad_out, (((0,), (0,)), ((), ())), preferred_element_type=jnp.float32
    )
    weight_total = lax.psum(weight_part, ("fam", "ctx"))
    weight_grad = weight_total * (lax.axis_size("fam") * ctx_size * tokens) ** (-0.5)
    return (
        query_grad.astype(jnp.bfloat16)[None],
        own_kgrad.astype(jnp.bfloat16)[None],
        own_vgrad.astype(jnp.bfloat16)[None],
        weight_grad,
    )


def solution(mesh):
    return jax.shard_map(
        per_device,
        mesh=mesh,
        in_specs=(
            P("fam", "ctx", None),
            P("fam", "ctx", None),
            P("fam", "ctx", None),
            P("fam", "ctx", None),
            P(),
            P("fam", None),
            P("fam", None),
            P("fam", None),
        ),
        out_specs=(P("fam", "ctx", None), P("fam", "ctx", None), P("fam", "ctx", None), P()),
        check_vma=False,
    )
```

profile of v0, /device:TPU:1, one launch (start us, length us, event | category | flops | bytes accessed | tf_op | source)
XLA Modules:
  0.0 967.8 jit_solution(17995845950725439622)
XLA Ops:
  11.3 4.6 collective-permute-start.1
  29.7 3.6 convolution_convert_fusion
  33.3 6.4 collective-permute-done
  44.0 19.9 %all-gather.7.cloned.1.call-done = bf16[512,1024]{1,0:T(8,128)(2,1)} async-done(((bf16[16,1024]{1,0:T(8,128)(2,1)}), bf16[512,1024]{1,0:T(8,128)(2,1)}) %all-gather.7.cloned.1.call-update) | async-done | bytes 1048592 | tf_op jit(solution)/shard_map/all_gather | solution.py:108
  63.9 44.9 %all-gather.5.cloned.1.call-done = bf16[512,1024]{1,0:T(8,128)(2,1)} async-done(((bf16[16,1024]{1,0:T(8,128)(2,1)}), bf16[512,1024]{1,0:T(8,128)(2,1)}) %all-gather.5.cloned.1.call-update) | async-done | bytes 1048592 | tf_op jit(solution)/shard_map/all_gather | solution.py:107
  118.0 518.4 %while.27 = (s32[]{:T(128)}, bf16[512,1024]{1,0:T(8,128)(2,1)}, f32[1024,1024]{1,0:T(8,128)}, f32[1024,1024]{1,0:T(8,128)}, f32[512,1024]{1,0:T(8,128)}, /*index...) while((s32[]{:T(128)}, bf16[512,1024]{1,0:T(8,128)(2,1)}, ...), condition=%wide.region_14.15_spmd, body=%wide.region_10.14_spmd.sunk | while | flops 1247747584 | bytes 80244984 | solution.py:200
  129.1 3.7 fusion.99
  132.8 7.0 fusion.100
  139.8 4.6 fusion.103
  144.4 13.6 %fusion.101 = bf16[2,64,512]{2,1,0:T(8,128)(2,1)S(1)} fusion(f32[2,512,1536]{2,1,0:T(8,128)} %fusion.99, bf16[512,2,64]{0,2,1:T(8,128)(2,1)S(1)} %bitcast.109, bf16[1024,2,64]{0,2,1:T(8,128)(2,1)S(1)} %bitcast.104, f32[2,512,1536]{2,1,0:T(8,128)} %get-tuple-element.467, f32[2,512]{1,0:T(2,128)S(1)} %broadcast_maximum_fusion.2), kind=kOutput, calls=%fused_computation.16.clone.1 | convolution fusion | flops 213125632 | bytes 13111296 | tf_op jit(solution)/shard_map/while/body/eval_jaxpr/gqk,kge->qge/dot_general | solution.py:75
  157.9 13.2 %fusion.102 = f32[1536,2,64]{0,2,1:T(8,128)S(1)} fusion(bf16[512,2,64]{0,2,1:T(8,128)(2,1)S(1)} %bitcast.107, f32[2,512,1536]{2,1,0:T(8,128)} %fusion.99, f32[2,512,1536]{2,1,0:T(8,128)} %get-tuple-element.467, f32[2,512]{1,0:T(2,128)S(1)} %broadcast_maximum_fusion.2), kind=kOutput, calls=%fused_computation.18.clone.1 | convolution fusion | flops 212339200 | bytes 13504512 | tf_op jit(solution)/shard_map/while/body/eval_jaxpr/gqk,qge->kge/dot_general | solution.py:76
  171.1 4.4 convolution_bitcast_fusion.2
  193.9 3.7 fusion.99
  197.6 7.0 fusion.100
  204.6 4.6 fusion.103
  209.2 13.6 %fusion.101 = bf16[2,64,512]{2,1,0:T(8,128)(2,1)S(1)} fusion(f32[2,512,1536]{2,1,0:T(8,128)} %fusion.99, bf16[512,2,64]{0,2,1:T(8,128)(2,1)S(1)} %bitcast.109, bf16[1024,2,64]{0,2,1:T(8,128)(2,1)S(1)} %bitcast.104, f32[2,512,1536]{2,1,0:T(8,128)} %get-tuple-element.467, f32[2,512]{1,0:T(2,128)S(1)} %broadcast_maximum_fusion.2), kind=kOutput, calls=%fused_computation.16.clone.1 | convolution fusion | flops 213125632 | bytes 13111296 | tf_op jit(solution)/shard_map/while/body/eval_jaxpr/gqk,kge->qge/dot_general | solution.py:75
  222.7 13.2 %fusion.102 = f32[1536,2,64]{0,2,1:T(8,128)S(1)} fusion(bf16[512,2,64]{0,2,1:T(8,128)(2,1)S(1)} %bitcast.107, f32[2,512,1536]{2,1,0:T(8,128)} %fusion.99, f32[2,512,1536]{2,1,0:T(8,128)} %get-tuple-element.467, f32[2,512]{1,0:T(2,128)S(1)} %broadcast_maximum_fusion.2), kind=kOutput, calls=%fused_computation.18.clone.1 | convolution fusion | flops 212339200 | bytes 13504512 | tf_op jit(solution)/shard_map/while/body/eval_jaxpr/gqk,qge->kge/dot_general | solution.py:76
  235.9 4.4 convolution_bitcast_fusion.2
  258.7 3.7 fusion.99
  262.4 7.0 fusion.100
  269.4 4.6 fusion.103
  274.0 13.6 %fusion.101 = bf16[2,64,512]{2,1,0:T(8,128)(2,1)S(1)} fusion(f32[2,512,1536]{2,1,0:T(8,128)} %fusion.99, bf16[512,2,64]{0,2,1:T(8,128)(2,1)S(1)} %bitcast.109, bf16[1024,2,64]{0,2,1:T(8,128)(2,1)S(1)} %bitcast.104, f32[2,512,1536]{2,1,0:T(8,128)} %get-tuple-element.467, f32[2,512]{1,0:T(2,128)S(1)} %broadcast_maximum_fusion.2), kind=kOutput, calls=%fused_computation.16.clone.1 | convolution fusion | flops 213125632 | bytes 13111296 | tf_op jit(solution)/shard_map/while/body/eval_jaxpr/gqk,kge->qge/dot_general | solution.py:75
  287.5 13.2 %fusion.102 = f32[1536,2,64]{0,2,1:T(8,128)S(1)} fusion(bf16[512,2,64]{0,2,1:T(8,128)(2,1)S(1)} %bitcast.107, f32[2,512,1536]{2,1,0:T(8,128)} %fusion.99, f32[2,512,1536]{2,1,0:T(8,128)} %get-tuple-element.467, f32[2,512]{1,0:T(2,128)S(1)} %broadcast_maximum_fusion.2), kind=kOutput, calls=%fused_computation.18.clone.1 | convolution fusion | flops 212339200 | bytes 13504512 | tf_op jit(solution)/shard_map/while/body/eval_jaxpr/gqk,qge->kge/dot_general | solution.py:76
  300.7 4.4 convolution_bitcast_fusion.2
  323.6 3.7 fusion.99
  327.2 7.0 fusion.100
  334.3 4.6 fusion.103
  338.8 13.6 %fusion.101 = bf16[2,64,512]{2,1,0:T(8,128)(2,1)S(1)} fusion(f32[2,512,1536]{2,1,0:T(8,128)} %fusion.99, bf16[512,2,64]{0,2,1:T(8,128)(2,1)S(1)} %bitcast.109, bf16[1024,2,64]{0,2,1:T(8,128)(2,1)S(1)} %bitcast.104, f32[2,512,1536]{2,1,0:T(8,128)} %get-tuple-element.467, f32[2,512]{1,0:T(2,128)S(1)} %broadcast_maximum_fusion.2), kind=kOutput, calls=%fused_computation.16.clone.1 | convolution fusion | flops 213125632 | bytes 13111296 | tf_op jit(solution)/shard_map/while/body/eval_jaxpr/gqk,kge->qge/dot_general | solution.py:75
  352.4 13.2 %fusion.102 = f32[1536,2,64]{0,2,1:T(8,128)S(1)} fusion(bf16[512,2,64]{0,2,1:T(8,128)(2,1)S(1)} %bitcast.107, f32[2,512,1536]{2,1,0:T(8,128)} %fusion.99, f32[2,512,1536]{2,1,0:T(8,128)} %get-tuple-element.467, f32[2,512]{1,0:T(2,128)S(1)} %broadcast_maximum_fusion.2), kind=kOutput, calls=%fused_computation.18.clone.1 | convolution fusion | flops 212339200 | bytes 13504512 | tf_op jit(solution)/shard_map/while/body/eval_jaxpr/gqk,qge->kge/dot_general | solution.py:76
  365.5 4.4 convolution_bitcast_fusion.2
  388.4 3.7 fusion.99
  392.0 7.0 fusion.100
  399.1 4.6 fusion.103
  403.6 13.6 %fusion.101 = bf16[2,64,512]{2,1,0:T(8,128)(2,1)S(1)} fusion(f32[2,512,1536]{2,1,0:T(8,128)} %fusion.99, bf16[512,2,64]{0,2,1:T(8,128)(2,1)S(1)} %bitcast.109, bf16[1024,2,64]{0,2,1:T(8,128)(2,1)S(1)} %bitcast.104, f32[2,512,1536]{2,1,0:T(8,128)} %get-tuple-element.467, f32[2,512]{1,0:T(2,128)S(1)} %broadcast_maximum_fusion.2), kind=kOutput, calls=%fused_computation.16.clone.1 | convolution fusion | flops 213125632 | bytes 13111296 | tf_op jit(solution)/shard_map/while/body/eval_jaxpr/gqk,kge->qge/dot_general | solution.py:75
  417.2 13.2 %fusion.102 = f32[1536,2,64]{0,2,1:T(8,128)S(1)} fusion(bf16[512,2,64]{0,2,1:T(8,128)(2,1)S(1)} %bitcast.107, f32[2,512,1536]{2,1,0:T(8,128)} %fusion.99, f32[2,512,1536]{2,1,0:T(8,128)} %get-tuple-element.467, f32[2,512]{1,0:T(2,128)S(1)} %broadcast_maximum_fusion.2), kind=kOutput, calls=%fused_computation.18.clone.1 | convolution fusion | flops 212339200 | bytes 13504512 | tf_op jit(solution)/shard_map/while/body/eval_jaxpr/gqk,qge->kge/dot_general | solution.py:76
  430.3 4.4 convolution_bitcast_fusion.2
  453.2 3.7 fusion.99
  456.9 7.0 fusion.100
  463.9 4.6 fusion.103
  468.4 13.6 %fusion.101 = bf16[2,64,512]{2,1,0:T(8,128)(2,1)S(1)} fusion(f32[2,512,1536]{2,1,0:T(8,128)} %fusion.99, bf16[512,2,64]{0,2,1:T(8,128)(2,1)S(1)} %bitcast.109, bf16[1024,2,64]{0,2,1:T(8,128)(2,1)S(1)} %bitcast.104, f32[2,512,1536]{2,1,0:T(8,128)} %get-tuple-element.467, f32[2,512]{1,0:T(2,128)S(1)} %broadcast_maximum_fusion.2), kind=kOutput, calls=%fused_computation.16.clone.1 | convolution fusion | flops 213125632 | bytes 13111296 | tf_op jit(solution)/shard_map/while/body/eval_jaxpr/gqk,kge->qge/dot_general | solution.py:75
  482.0 13.2 %fusion.102 = f32[1536,2,64]{0,2,1:T(8,128)S(1)} fusion(bf16[512,2,64]{0,2,1:T(8,128)(2,1)S(1)} %bitcast.107, f32[2,512,1536]{2,1,0:T(8,128)} %fusion.99, f32[2,512,1536]{2,1,0:T(8,128)} %get-tuple-element.467, f32[2,512]{1,0:T(2,128)S(1)} %broadcast_maximum_fusion.2), kind=kOutput, calls=%fused_computation.18.clone.1 | convolution fusion | flops 212339200 | bytes 13504512 | tf_op jit(solution)/shard_map/while/body/eval_jaxpr/gqk,qge->kge/dot_general | solution.py:76
  495.1 4.4 convolution_bitcast_fusion.2
  518.0 3.7 fusion.99
  521.6 7.0 fusion.100
  528.6 4.6 fusion.103
  533.2 13.6 %fusion.101 = bf16[2,64,512]{2,1,0:T(8,128)(2,1)S(1)} fusion(f32[2,512,1536]{2,1,0:T(8,128)} %fusion.99, bf16[512,2,64]{0,2,1:T(8,128)(2,1)S(1)} %bitcast.109, bf16[1024,2,64]{0,2,1:T(8,128)(2,1)S(1)} %bitcast.104, f32[2,512,1536]{2,1,0:T(8,128)} %get-tuple-element.467, f32[2,512]{1,0:T(2,128)S(1)} %broadcast_maximum_fusion.2), kind=kOutput, calls=%fused_computation.16.clone.1 | convolution fusion | flops 213125632 | bytes 13111296 | tf_op jit(solution)/shard_map/while/body/eval_jaxpr/gqk,kge->qge/dot_general | solution.py:75
  546.8 13.2 %fusion.102 = f32[1536,2,64]{0,2,1:T(8,128)S(1)} fusion(bf16[512,2,64]{0,2,1:T(8,128)(2,1)S(1)} %bitcast.107, f32[2,512,1536]{2,1,0:T(8,128)} %fusion.99, f32[2,512,1536]{2,1,0:T(8,128)} %get-tuple-element.467, f32[2,512]{1,0:T(2,128)S(1)} %broadcast_maximum_fusion.2), kind=kOutput, calls=%fused_computation.18.clone.1 | convolution fusion | flops 212339200 | bytes 13504512 | tf_op jit(solution)/shard_map/while/body/eval_jaxpr/gqk,qge->kge/dot_general | solution.py:76
  559.9 4.4 convolution_bitcast_fusion.2
  582.7 3.7 fusion.99
  586.4 7.0 fusion.100
  593.4 4.6 fusion.103
  598.0 13.6 %fusion.101 = bf16[2,64,512]{2,1,0:T(8,128)(2,1)S(1)} fusion(f32[2,512,1536]{2,1,0:T(8,128)} %fusion.99, bf16[512,2,64]{0,2,1:T(8,128)(2,1)S(1)} %bitcast.109, bf16[1024,2,64]{0,2,1:T(8,128)(2,1)S(1)} %bitcast.104, f32[2,512,1536]{2,1,0:T(8,128)} %get-tuple-element.467, f32[2,512]{1,0:T(2,128)S(1)} %broadcast_maximum_fusion.2), kind=kOutput, calls=%fused_computation.16.clone.1 | convolution fusion | flops 213125632 | bytes 13111296 | tf_op jit(solution)/shard_map/while/body/eval_jaxpr/gqk,kge->qge/dot_general | solution.py:75
  611.6 13.2 %fusion.102 = f32[1536,2,64]{0,2,1:T(8,128)S(1)} fusion(bf16[512,2,64]{0,2,1:T(8,128)(2,1)S(1)} %bitcast.107, f32[2,512,1536]{2,1,0:T(8,128)} %fusion.99, f32[2,512,1536]{2,1,0:T(8,128)} %get-tuple-element.467, f32[2,512]{1,0:T(2,128)S(1)} %broadcast_maximum_fusion.2), kind=kOutput, calls=%fused_computation.18.clone.1 | convolution fusion | flops 212339200 | bytes 13504512 | tf_op jit(solution)/shard_map/while/body/eval_jaxpr/gqk,qge->kge/dot_general | solution.py:76
  624.7 4.4 convolution_bitcast_fusion.2
  636.4 3.0 convert_element_type.75
  644.8 4.8 fusion.41
  653.6 5.0 collective-permute-done.3
  660.6 9.2 collective-permute-done.2
  671.4 43.8 %reduce-scatter.5.cloned.1.call-done = bf16[16,1024]{1,0:T(8,128)(2,1)} async-done(((bf16[512,1024]{1,0:T(8,128)(2,1)}), bf16[16,1024]{1,0:T(8,128)(2,1)}) %reduce-scatter.5.cloned.1.call-update) | async-done | bytes 32784 | tf_op jit(solution)/shard_map/reduce_scatter | solution.py:213
  716.9 79.4 %reduce-scatter.3.cloned.1.call-done = bf16[16,1024]{1,0:T(8,128)(2,1)} async-done(((bf16[512,1024]{1,0:T(8,128)(2,1)}), bf16[16,1024]{1,0:T(8,128)(2,1)}) %reduce-scatter.3.cloned.1.call-update) | async-done | bytes 32784 | tf_op jit(solution)/shard_map/reduce_scatter | solution.py:210
  796.3 3.8 scatter_custom_fusion
  801.3 2.9 convert_bitcast_fusion.1
  804.2 152.1 %all-reduce.2.cloned.1.call-done = f32[1024,1024]{1,0:T(8,128)} async-done(((f32[1024,1024]{1,0:T(8,128)}), f32[1024,1024]{1,0:T(8,128)}) %all-reduce.2.cloned.1.call-update) | async-done | bytes 4194320 | tf_op jit(solution)/shard_map/psum | solution.py:222
  956.3 5.0 broadcast_multiply_fusion
  (363 shorter events, 193.2 us)
Async XLA Ops:
  7.2 22.5 %copy-start = (bf16[1024,1024]{1,0:T(8,128)(2,1)S(1)}, bf16[1024,1024]{1,0:T(8,128)(2,1)}, u32[]{:S(2)}) copy-start(bf16[1024,1024]{1,0:T(8,128)(2,1)} %param.22) | copy-start | bytes 6291460
  7.2 56.7 %all-gather.7.cloned.1.call-start = ((), (), s32[]{:S(2)}) async-start(), calls=%async_computation.6 | async-start | bytes 1081344 | tf_op jit(solution)/shard_map/all_gather | solution.py:108
  8.1 0.5 copy-start.6
  11.2 97.5 %all-gather.5.cloned.1.call-start = ((), (), s32[]{:S(2)}) async-start(), calls=%async_computation.5 | async-start | bytes 1081344 | tf_op jit(solution)/shard_map/all_gather | solution.py:107
  11.3 31.3 %collective-permute-start.1 = (bf16[512,1024]{1,0:T(8,128)(2,1)}, bf16[512,1024]{1,0:T(8,128)(2,1)S(1)}, u32[]{:S(2)}, u32[]{:S(2)}) collective-permute-start(bf16[512,1024]{1,0:T(8,128)(2,1)} %bitcast.115), channel_id=1, source_target_pairs={{0,1},{1,2},{2,3},{3,4},{4,5},{5,6},{6,7},{7,8},{8,9},{9,10},{10,1... | collective-permute-start | bytes 3145736 | tf_op jit(solution)/shard_map/ppermute | solution.py:15
  15.9 23.8 %collective-permute-start = (bf16[512,1024]{1,0:T(8,128)(2,1)}, bf16[512,1024]{1,0:T(8,128)(2,1)}, u32[]{:S(2)}, u32[]{:S(2)}) collective-permute-start(bf16[512,1024]{1,0:T(8,128)(2,1)} %bitcast.111), channel_id=1, source_target_pairs={{0,1},{1,2},{2,3},{3,4},{4,5},{5,6},{6,7},{7,8},{8,9},{9,10},{10,1... | collective-permute-start | bytes 3145736 | tf_op jit(solution)/shard_map/ppermute | solution.py:15
  20.4 694.8 %reduce-scatter.5.cloned.1.call-start = ((), (), s32[]{:S(2)}) async-start(), calls=%async_computation.3 | async-start | bytes 1081344 | tf_op jit(solution)/shard_map/reduce_scatter | solution.py:213
  29.7 10.0 %copy-start.4 = (bf16[1,512,1024]{2,1,0:T(8,128)(2,1)S(1)}, bf16[1,512,1024]{2,1,0:T(8,128)(2,1)}, u32[]{:S(2)}) copy-start(bf16[1,512,1024]{2,1,0:T(8,128)(2,1)} %param.19) | copy-start | bytes 3145732
  33.3 9.3 copy-start.5
  636.4 3.1 copy-start.3
  639.4 156.9 %reduce-scatter.3.cloned.1.call-start = ((), (), s32[]{:S(2)}) async-start(), calls=%async_computation.2 | async-start | bytes 1081344 | tf_op jit(solution)/shard_map/reduce_scatter | solution.py:210
  640.7 315.6 %all-reduce.2.cloned.1.call-start = ((), (), s32[]{:S(2)}) async-start(), calls=%async_computation.4 | async-start | bytes 8388608 | tf_op jit(solution)/shard_map/psum | solution.py:222
  642.5 16.1 %collective-permute-start.3 = (bf16[512,1024]{1,0:T(8,128)(2,1)S(1)}, bf16[512,1024]{1,0:T(8,128)(2,1)S(1)}, u32[]{:S(2)}, u32[]{:S(2)}) collective-permute-start(bf16[512,1024]{1,0:T(8,128)(2,1)S(1)} %slice.88), channel_id=1, source_target_pairs={{1,0},{2,1},{3,2},{4,3},{5,4},{6,5},{7,6},{8,7},{9,8},{10,9},{11,1... | collective-permute-start | bytes 3145736 | tf_op jit(solution)/shard_map/ppermute | solution.py:15
  649.6 20.2 %copy-start.2 = (f32[1024,1024]{1,0:T(8,128)S(1)}, f32[1024,1024]{1,0:T(8,128)}, u32[]{:S(2)}) copy-start(f32[1024,1024]{1,0:T(8,128)} %get-tuple-element.279) | copy-start | bytes 12582916
  651.6 18.3 %collective-permute-start.2 = (bf16[512,1024]{1,0:T(8,128)(2,1)S(1)}, bf16[512,1024]{1,0:T(8,128)(2,1)S(1)}, u32[]{:S(2)}, u32[]{:S(2)}) collective-permute-start(bf16[512,1024]{1,0:T(8,128)(2,1)S(1)} %slice.89), channel_id=1, source_target_pairs={{1,0},{2,1},{3,2},{4,3},{5,4},{6,5},{7,6},{8,7},{9,8},{10,9},{11,1... | collective-permute-start | bytes 3145736 | tf_op jit(solution)/shard_map/ppermute | solution.py:15
  801.3 160.0 %copy-start.1 = (bf16[1024,1024]{1,0:T(8,128)(2,1)S(1)}, bf16[1024,1024]{1,0:T(8,128)(2,1)}, u32[]{:S(2)}) copy-start(bf16[1024,1024]{1,0:T(8,128)(2,1)} %param.22) | copy-start | bytes 6291460
Sparse Core Ops, SparseCore 0:
  11.4 52.4 all-gather.6
  66.7 41.9 all-gather.4
  639.6 75.6 reduce-scatter.4
  719.5 76.7 reduce-scatter.2
  801.1 155.0 all-reduce.1
where the time goes:
time: 972 us; the launch traced here: 968 us
  matrix products  379 us (39%)
  waiting for transfers between devices  361 us (37%)
  local copies, waits for them, and re-layouts  166 us (17%)
  other arithmetic  35.4 us (4%)
  between operations  13.9 us (1%)
  starting transfers between devices  11.1 us (1%)
    psum x1, waiting for transfers between devices, per_device(): weight_total = lax.psum(weight_part, ('fam', 'ctx'))  152 us
    dot_general x8, matrix products, attend(): jnp.einsum('gqk,kge->qge', grad_score, key_blk, preferred_element_type=jn...  108 us
    dot_general x8, matrix products, attend(): jnp.einsum('gqk,qge->kge', grad_score, query_blk, preferred_element_type=...  105 us
    reduce_scatter x1, waiting for transfers between devices, per_device(): lax.psum_scatter(mem_kgrad.astype(jnp.bfloat16), 'ctx', scatter_dimension...  79.4 us
    sub x8, matrix products, attend(): expo = jnp.where(live, jnp.exp(shifted - row_max), 0.0)  56 us
    dynamic_slice x88, local copies, waits for them, and re-layouts, columns_of(): return lax.dynamic_slice_in_dim(array, column, span, 1)  50 us
    all_gather x1, waiting for transfers between devices, per_device(): lax.all_gather(key_loc[own_slots], 'ctx', axis=0, tiled=True)  44.9 us
    reduce_scatter x1, waiting for transfers between devices, per_device(): lax.psum_scatter(mem_vgrad.astype(jnp.bfloat16), 'ctx', scatter_dimension...  43.8 us
  transfers between devices with their start and end apart: 9, of which 8 were waited for; matrix products, arithmetic and copies ran while one was open for 4% of the time, Pallas kernels for 0%

commit v1 on v0

--- a/solution.py
+++ b/solution.py
@@ -219,7 +219,7 @@
     weight_part = lax.dot_general(
         attn_rows, grad_out, (((0,), (0,)), ((), ())), preferred_element_type=jnp.float32
     )
-    weight_total = lax.psum(weight_part, ("fam", "ctx"))
+    weight_total = lax.psum(lax.psum(weight_part, "fam"), "ctx")
     weight_grad = weight_total * (lax.axis_size("fam") * ctx_size * tokens) ** (-0.5)
     return (
         query_grad.astype(jnp.bfloat16)[None],

time: 972 us -> 1030 us (1.060)
  waiting for transfers between devices: 361 us -> 413 us
    psum x1 -> x2, waiting for transfers between devices: 152 us -> 191 us  [per_device(): weight_total = lax.psum(lax.psum(weight_part, 'fam'), 'ctx')]
    reduce_scatter x1, waiting for transfers between devices: 43.8 us -> 60.1 us  [per_device(): lax.psum_scatter(mem_vgrad.astype(jnp.bfloat16), 'ctx', scatter_dimension...]
  transfers between devices with their start and end apart: 9 -> 10, of which waited for: 8 -> 8; matrix products, arithmetic and copies ran while one was open for 4% -> 4% of each run, Pallas kernels for 0% -> 0%
where the time goes in v1:
time: 1030 us; the launch traced here: 1020 us
  waiting for transfers between devices  413 us (40%)
  matrix products  379 us (37%)
  local copies, waits for them, and re-layouts  167 us (16%)
  other arithmetic  35.1 us (3%)
  between operations  14.3 us (1%)
  starting transfers between devices  11.5 us (1%)
    psum x2, waiting for transfers between devices, per_device(): weight_total = lax.psum(lax.psum(weight_part, 'fam'), 'ctx')  191 us
    dot_general x8, matrix products, attend(): jnp.einsum('gqk,kge->qge', grad_score, key_blk, preferred_element_type=jn...  108 us
    dot_general x8, matrix products, attend(): jnp.einsum('gqk,qge->kge', grad_score, query_blk, preferred_element_type=...  105 us
    reduce_scatter x1, waiting for transfers between devices, per_device(): lax.psum_scatter(mem_kgrad.astype(jnp.bfloat16), 'ctx', scatter_dimension...  79 us
    reduce_scatter x1, waiting for transfers between devices, per_device(): lax.psum_scatter(mem_vgrad.astype(jnp.bfloat16), 'ctx', scatter_dimension...  60.1 us
    sub x8, matrix products, attend(): expo = jnp.where(live, jnp.exp(shifted - row_max), 0.0)  56 us
    dynamic_slice x88, local copies, waits for them, and re-layouts, columns_of(): return lax.dynamic_slice_in_dim(array, column, span, 1)  50 us
    all_gather x1, waiting for transfers between devices, per_device(): lax.all_gather(key_loc[own_slots], 'ctx', axis=0, tiled=True)  44.9 us
  transfers between devices with their start and end apart: 10, of which 8 were waited for; matrix products, arithmetic and copies ran while one was open for 4% of the time, Pallas kernels for 0%

profile of v1, /device:TPU:1, one launch (start us, length us, event | category | flops | bytes accessed | tf_op | source)
XLA Modules:
  0.0 1021.9 jit_solution(18279666372157138422)
XLA Ops:
  11.3 4.6 collective-permute-start.1
  29.7 3.6 convolution_convert_fusion
  33.3 6.4 collective-permute-done
  39.7 2.8 pad_maximum_fusion.10
  44.0 19.9 %all-gather.7.cloned.1.call-done = bf16[512,1024]{1,0:T(8,128)(2,1)} async-done(((bf16[16,1024]{1,0:T(8,128)(2,1)}), bf16[512,1024]{1,0:T(8,128)(2,1)}) %all-gather.7.cloned.1.call-update) | async-done | bytes 1048592 | tf_op jit(solution)/shard_map/all_gather | solution.py:108
  63.9 44.9 %all-gather.5.cloned.1.call-done = bf16[512,1024]{1,0:T(8,128)(2,1)} async-done(((bf16[16,1024]{1,0:T(8,128)(2,1)}), bf16[512,1024]{1,0:T(8,128)(2,1)}) %all-gather.5.cloned.1.call-update) | async-done | bytes 1048592 | tf_op jit(solution)/shard_map/all_gather | solution.py:107
  118.0 518.4 %while.27 = (s32[]{:T(128)}, bf16[512,1024]{1,0:T(8,128)(2,1)}, f32[1024,1024]{1,0:T(8,128)}, f32[1024,1024]{1,0:T(8,128)}, f32[512,1024]{1,0:T(8,128)}, /*index...) while((s32[]{:T(128)}, bf16[512,1024]{1,0:T(8,128)(2,1)}, ...), condition=%wide.region_14.15_spmd, body=%wide.region_10.14_spmd.sunk | while | flops 1247747584 | bytes 80244984 | solution.py:200
  129.1 3.7 fusion.99
  132.8 7.0 fusion.100
  139.8 4.6 fusion.103
  144.4 13.6 %fusion.101 = bf16[2,64,512]{2,1,0:T(8,128)(2,1)S(1)} fusion(f32[2,512,1536]{2,1,0:T(8,128)} %fusion.99, bf16[512,2,64]{0,2,1:T(8,128)(2,1)S(1)} %bitcast.109, bf16[1024,2,64]{0,2,1:T(8,128)(2,1)S(1)} %bitcast.104, f32[2,512,1536]{2,1,0:T(8,128)} %get-tuple-element.467, f32[2,512]{1,0:T(2,128)S(1)} %broadcast_maximum_fusion.2), kind=kOutput, calls=%fused_computation.16.clone.1 | convolution fusion | flops 213125632 | bytes 13111296 | tf_op jit(solution)/shard_map/while/body/eval_jaxpr/gqk,kge->qge/dot_general | solution.py:75
  157.9 13.2 %fusion.102 = f32[1536,2,64]{0,2,1:T(8,128)S(1)} fusion(bf16[512,2,64]{0,2,1:T(8,128)(2,1)S(1)} %bitcast.107, f32[2,512,1536]{2,1,0:T(8,128)} %fusion.99, f32[2,512,1536]{2,1,0:T(8,128)} %get-tuple-element.467, f32[2,512]{1,0:T(2,128)S(1)} %broadcast_maximum_fusion.2), kind=kOutput, calls=%fused_computation.18.clone.1 | convolution fusion | flops 212339200 | bytes 13504512 | tf_op jit(solution)/shard_map/while/body/eval_jaxpr/gqk,qge->kge/dot_general | solution.py:76
  171.1 4.4 convolution_bitcast_fusion.2
  193.9 3.7 fusion.99
  197.6 7.0 fusion.100
  204.6 4.6 fusion.103
  209.2 13.6 %fusion.101 = bf16[2,64,512]{2,1,0:T(8,128)(2,1)S(1)} fusion(f32[2,512,1536]{2,1,0:T(8,128)} %fusion.99, bf16[512,2,64]{0,2,1:T(8,128)(2,1)S(1)} %bitcast.109, bf16[1024,2,64]{0,2,1:T(8,128)(2,1)S(1)} %bitcast.104, f32[2,512,1536]{2,1,0:T(8,128)} %get-tuple-element.467, f32[2,512]{1,0:T(2,128)S(1)} %broadcast_maximum_fusion.2), kind=kOutput, calls=%fused_computation.16.clone.1 | convolution fusion | flops 213125632 | bytes 13111296 | tf_op jit(solution)/shard_map/while/body/eval_jaxpr/gqk,kge->qge/dot_general | solution.py:75
  222.7 13.2 %fusion.102 = f32[1536,2,64]{0,2,1:T(8,128)S(1)} fusion(bf16[512,2,64]{0,2,1:T(8,128)(2,1)S(1)} %bitcast.107, f32[2,512,1536]{2,1,0:T(8,128)} %fusion.99, f32[2,512,1536]{2,1,0:T(8,128)} %get-tuple-element.467, f32[2,512]{1,0:T(2,128)S(1)} %broadcast_maximum_fusion.2), kind=kOutput, calls=%fused_computation.18.clone.1 | convolution fusion | flops 212339200 | bytes 13504512 | tf_op jit(solution)/shard_map/while/body/eval_jaxpr/gqk,qge->kge/dot_general | solution.py:76
  235.9 4.4 convolution_bitcast_fusion.2
  258.7 3.7 fusion.99
  262.4 7.0 fusion.100
  269.4 4.6 fusion.103
  274.0 13.6 %fusion.101 = bf16[2,64,512]{2,1,0:T(8,128)(2,1)S(1)} fusion(f32[2,512,1536]{2,1,0:T(8,128)} %fusion.99, bf16[512,2,64]{0,2,1:T(8,128)(2,1)S(1)} %bitcast.109, bf16[1024,2,64]{0,2,1:T(8,128)(2,1)S(1)} %bitcast.104, f32[2,512,1536]{2,1,0:T(8,128)} %get-tuple-element.467, f32[2,512]{1,0:T(2,128)S(1)} %broadcast_maximum_fusion.2), kind=kOutput, calls=%fused_computation.16.clone.1 | convolution fusion | flops 213125632 | bytes 13111296 | tf_op jit(solution)/shard_map/while/body/eval_jaxpr/gqk,kge->qge/dot_general | solution.py:75
  287.5 13.2 %fusion.102 = f32[1536,2,64]{0,2,1:T(8,128)S(1)} fusion(bf16[512,2,64]{0,2,1:T(8,128)(2,1)S(1)} %bitcast.107, f32[2,512,1536]{2,1,0:T(8,128)} %fusion.99, f32[2,512,1536]{2,1,0:T(8,128)} %get-tuple-element.467, f32[2,512]{1,0:T(2,128)S(1)} %broadcast_maximum_fusion.2), kind=kOutput, calls=%fused_computation.18.clone.1 | convolution fusion | flops 212339200 | bytes 13504512 | tf_op jit(solution)/shard_map/while/body/eval_jaxpr/gqk,qge->kge/dot_general | solution.py:76
  300.7 4.4 convolution_bitcast_fusion.2
  323.6 3.7 fusion.99
  327.2 7.0 fusion.100
  334.3 4.6 fusion.103
  338.8 13.6 %fusion.101 = bf16[2,64,512]{2,1,0:T(8,128)(2,1)S(1)} fusion(f32[2,512,1536]{2,1,0:T(8,128)} %fusion.99, bf16[512,2,64]{0,2,1:T(8,128)(2,1)S(1)} %bitcast.109, bf16[1024,2,64]{0,2,1:T(8,128)(2,1)S(1)} %bitcast.104, f32[2,512,1536]{2,1,0:T(8,128)} %get-tuple-element.467, f32[2,512]{1,0:T(2,128)S(1)} %broadcast_maximum_fusion.2), kind=kOutput, calls=%fused_computation.16.clone.1 | convolution fusion | flops 213125632 | bytes 13111296 | tf_op jit(solution)/shard_map/while/body/eval_jaxpr/gqk,kge->qge/dot_general | solution.py:75
  352.4 13.2 %fusion.102 = f32[1536,2,64]{0,2,1:T(8,128)S(1)} fusion(bf16[512,2,64]{0,2,1:T(8,128)(2,1)S(1)} %bitcast.107, f32[2,512,1536]{2,1,0:T(8,128)} %fusion.99, f32[2,512,1536]{2,1,0:T(8,128)} %get-tuple-element.467, f32[2,512]{1,0:T(2,128)S(1)} %broadcast_maximum_fusion.2), kind=kOutput, calls=%fused_computation.18.clone.1 | convolution fusion | flops 212339200 | bytes 13504512 | tf_op jit(solution)/shard_map/while/body/eval_jaxpr/gqk,qge->kge/dot_general | solution.py:76
  365.5 4.4 convolution_bitcast_fusion.2
  388.4 3.7 fusion.99
  392.0 7.0 fusion.100
  399.1 4.6 fusion.103
  403.6 13.6 %fusion.101 = bf16[2,64,512]{2,1,0:T(8,128)(2,1)S(1)} fusion(f32[2,512,1536]{2,1,0:T(8,128)} %fusion.99, bf16[512,2,64]{0,2,1:T(8,128)(2,1)S(1)} %bitcast.109, bf16[1024,2,64]{0,2,1:T(8,128)(2,1)S(1)} %bitcast.104, f32[2,512,1536]{2,1,0:T(8,128)} %get-tuple-element.467, f32[2,512]{1,0:T(2,128)S(1)} %broadcast_maximum_fusion.2), kind=kOutput, calls=%fused_computation.16.clone.1 | convolution fusion | flops 213125632 | bytes 13111296 | tf_op jit(solution)/shard_map/while/body/eval_jaxpr/gqk,kge->qge/dot_general | solution.py:75
  417.2 13.2 %fusion.102 = f32[1536,2,64]{0,2,1:T(8,128)S(1)} fusion(bf16[512,2,64]{0,2,1:T(8,128)(2,1)S(1)} %bitcast.107, f32[2,512,1536]{2,1,0:T(8,128)} %fusion.99, f32[2,512,1536]{2,1,0:T(8,128)} %get-tuple-element.467, f32[2,512]{1,0:T(2,128)S(1)} %broadcast_maximum_fusion.2), kind=kOutput, calls=%fused_computation.18.clone.1 | convolution fusion | flops 212339200 | bytes 13504512 | tf_op jit(solution)/shard_map/while/body/eval_jaxpr/gqk,qge->kge/dot_general | solution.py:76
  430.3 4.4 convolution_bitcast_fusion.2
  453.2 3.7 fusion.99
  456.9 7.0 fusion.100
  463.9 4.6 fusion.103
  468.4 13.6 %fusion.101 = bf16[2,64,512]{2,1,0:T(8,128)(2,1)S(1)} fusion(f32[2,512,1536]{2,1,0:T(8,128)} %fusion.99, bf16[512,2,64]{0,2,1:T(8,128)(2,1)S(1)} %bitcast.109, bf16[1024,2,64]{0,2,1:T(8,128)(2,1)S(1)} %bitcast.104, f32[2,512,1536]{2,1,0:T(8,128)} %get-tuple-element.467, f32[2,512]{1,0:T(2,128)S(1)} %broadcast_maximum_fusion.2), kind=kOutput, calls=%fused_computation.16.clone.1 | convolution fusion | flops 213125632 | bytes 13111296 | tf_op jit(solution)/shard_map/while/body/eval_jaxpr/gqk,kge->qge/dot_general | solution.py:75
  482.0 13.2 %fusion.102 = f32[1536,2,64]{0,2,1:T(8,128)S(1)} fusion(bf16[512,2,64]{0,2,1:T(8,128)(2,1)S(1)} %bitcast.107, f32[2,512,1536]{2,1,0:T(8,128)} %fusion.99, f32[2,512,1536]{2,1,0:T(8,128)} %get-tuple-element.467, f32[2,512]{1,0:T(2,128)S(1)} %broadcast_maximum_fusion.2), kind=kOutput, calls=%fused_computation.18.clone.1 | convolution fusion | flops 212339200 | bytes 13504512 | tf_op jit(solution)/shard_map/while/body/eval_jaxpr/gqk,qge->kge/dot_general | solution.py:76
  495.1 4.4 convolution_bitcast_fusion.2
  518.0 3.7 fusion.99
  521.6 7.0 fusion.100
  528.6 4.6 fusion.103
  533.2 13.6 %fusion.101 = bf16[2,64,512]{2,1,0:T(8,128)(2,1)S(1)} fusion(f32[2,512,1536]{2,1,0:T(8,128)} %fusion.99, bf16[512,2,64]{0,2,1:T(8,128)(2,1)S(1)} %bitcast.109, bf16[1024,2,64]{0,2,1:T(8,128)(2,1)S(1)} %bitcast.104, f32[2,512,1536]{2,1,0:T(8,128)} %get-tuple-element.467, f32[2,512]{1,0:T(2,128)S(1)} %broadcast_maximum_fusion.2), kind=kOutput, calls=%fused_computation.16.clone.1 | convolution fusion | flops 213125632 | bytes 13111296 | tf_op jit(solution)/shard_map/while/body/eval_jaxpr/gqk,kge->qge/dot_general | solution.py:75
  546.8 13.2 %fusion.102 = f32[1536,2,64]{0,2,1:T(8,128)S(1)} fusion(bf16[512,2,64]{0,2,1:T(8,128)(2,1)S(1)} %bitcast.107, f32[2,512,1536]{2,1,0:T(8,128)} %fusion.99, f32[2,512,1536]{2,1,0:T(8,128)} %get-tuple-element.467, f32[2,512]{1,0:T(2,128)S(1)} %broadcast_maximum_fusion.2), kind=kOutput, calls=%fused_computation.18.clone.1 | convolution fusion | flops 212339200 | bytes 13504512 | tf_op jit(solution)/shard_map/while/body/eval_jaxpr/gqk,qge->kge/dot_general | solution.py:76
  559.9 4.4 convolution_bitcast_fusion.2
  582.7 3.7 fusion.99
  586.4 7.0 fusion.100
  593.4 4.6 fusion.103
  598.0 13.6 %fusion.101 = bf16[2,64,512]{2,1,0:T(8,128)(2,1)S(1)} fusion(f32[2,512,1536]{2,1,0:T(8,128)} %fusion.99, bf16[512,2,64]{0,2,1:T(8,128)(2,1)S(1)} %bitcast.109, bf16[1024,2,64]{0,2,1:T(8,128)(2,1)S(1)} %bitcast.104, f32[2,512,1536]{2,1,0:T(8,128)} %get-tuple-element.467, f32[2,512]{1,0:T(2,128)S(1)} %broadcast_maximum_fusion.2), kind=kOutput, calls=%fused_computation.16.clone.1 | convolution fusion | flops 213125632 | bytes 13111296 | tf_op jit(solution)/shard_map/while/body/eval_jaxpr/gqk,kge->qge/dot_general | solution.py:75
  611.6 13.2 %fusion.102 = f32[1536,2,64]{0,2,1:T(8,128)S(1)} fusion(bf16[512,2,64]{0,2,1:T(8,128)(2,1)S(1)} %bitcast.107, f32[2,512,1536]{2,1,0:T(8,128)} %fusion.99, f32[2,512,1536]{2,1,0:T(8,128)} %get-tuple-element.467, f32[2,512]{1,0:T(2,128)S(1)} %broadcast_maximum_fusion.2), kind=kOutput, calls=%fused_computation.18.clone.1 | convolution fusion | flops 212339200 | bytes 13504512 | tf_op jit(solution)/shard_map/while/body/eval_jaxpr/gqk,qge->kge/dot_general | solution.py:76
  624.7 4.4 convolution_bitcast_fusion.2
  636.4 4.8 fusion.41
  650.7 82.7 %all-reduce.3.cloned.1.call-done = f32[1024,1024]{1,0:T(8,128)} async-done(((f32[1024,1024]{1,0:T(8,128)}), f32[1024,1024]{1,0:T(8,128)}) %all-reduce.3.cloned.1.call-update) | async-done | bytes 4194320 | tf_op jit(solution)/shard_map/psum | solution.py:222
  740.0 11.5 %collective-permute-done.2 = bf16[512,1024]{1,0:T(8,128)(2,1)S(1)} collective-permute-done((bf16[512,1024]{1,0:T(8,128)(2,1)S(1)}, bf16[512,1024]{1,0:T(8,128)(2,1)S(1)}, u32[]{:S(2)}, u32[]{:S(2)}) %collective-permute-start.2) | collective-permute-done | bytes 1048608 | tf_op jit(solution)/shard_map/ppermute | solution.py:15
  753.1 60.1 %reduce-scatter.5.cloned.1.call-done = bf16[16,1024]{1,0:T(8,128)(2,1)} async-done(((bf16[512,1024]{1,0:T(8,128)(2,1)}), bf16[16,1024]{1,0:T(8,128)(2,1)}) %reduce-scatter.5.cloned.1.call-update) | async-done | bytes 32784 | tf_op jit(solution)/shard_map/reduce_scatter | solution.py:213
  815.0 79.0 %reduce-scatter.3.cloned.1.call-done = bf16[16,1024]{1,0:T(8,128)(2,1)} async-done(((bf16[512,1024]{1,0:T(8,128)(2,1)}), bf16[16,1024]{1,0:T(8,128)(2,1)}) %reduce-scatter.3.cloned.1.call-update) | async-done | bytes 32784 | tf_op jit(solution)/shard_map/reduce_scatter | solution.py:210
  894.0 3.8 scatter_custom_fusion
  898.9 2.9 convert_bitcast_fusion.1
  901.8 108.2 %all-reduce.5.cloned.1.call-done = f32[1024,1024]{1,0:T(8,128)} async-done(((f32[1024,1024]{1,0:T(8,128)}), f32[1024,1024]{1,0:T(8,128)}) %all-reduce.5.cloned.1.call-update) | async-done | bytes 4194320 | tf_op jit(solution)/shard_map/psum | solution.py:222
  1010.0 5.0 broadcast_multiply_fusion
  (366 shorter events, 194.9 us)
Async XLA Ops:
  7.2 22.5 %copy-start = (bf16[1024,1024]{1,0:T(8,128)(2,1)S(1)}, bf16[1024,1024]{1,0:T(8,128)(2,1)}, u32[]{:S(2)}) copy-start(bf16[1024,1024]{1,0:T(8,128)(2,1)} %param.22) | copy-start | bytes 6291460
  7.2 56.7 %all-gather.7.cloned.1.call-start = ((), (), s32[]{:S(2)}) async-start(), calls=%async_computation.7 | async-start | bytes 1081344 | tf_op jit(solution)/shard_map/all_gather | solution.py:108
  8.1 0.5 copy-start.6
  11.2 97.5 %all-gather.5.cloned.1.call-start = ((), (), s32[]{:S(2)}) async-start(), calls=%async_computation.6 | async-start | bytes 1081344 | tf_op jit(solution)/shard_map/all_gather | solution.py:107
  11.3 31.3 %collective-permute-start.1 = (bf16[512,1024]{1,0:T(8,128)(2,1)}, bf16[512,1024]{1,0:T(8,128)(2,1)S(1)}, u32[]{:S(2)}, u32[]{:S(2)}) collective-permute-start(bf16[512,1024]{1,0:T(8,128)(2,1)} %bitcast.115), channel_id=1, source_target_pairs={{0,1},{1,2},{2,3},{3,4},{4,5},{5,6},{6,7},{7,8},{8,9},{9,10},{10,1... | collective-permute-start | bytes 3145736 | tf_op jit(solution)/shard_map/ppermute | solution.py:15
  15.9 23.8 %collective-permute-start = (bf16[512,1024]{1,0:T(8,128)(2,1)}, bf16[512,1024]{1,0:T(8,128)(2,1)}, u32[]{:S(2)}, u32[]{:S(2)}) collective-permute-start(bf16[512,1024]{1,0:T(8,128)(2,1)} %bitcast.111), channel_id=1, source_target_pairs={{0,1},{1,2},{2,3},{3,4},{4,5},{5,6},{6,7},{7,8},{8,9},{9,10},{10,1... | collective-permute-start | bytes 3145736 | tf_op jit(solution)/shard_map/ppermute | solution.py:15
  20.4 713.0 %all-reduce.3.cloned.1.call-start = ((), (), s32[]{:S(2)}) async-start(), calls=%async_computation.4 | async-start | bytes 8388608 | tf_op jit(solution)/shard_map/psum | solution.py:222
  29.7 10.0 copy-start.4
  33.3 9.3 copy-start.5
  641.2 1.6 copy-start.3
  641.2 172.0 %reduce-scatter.5.cloned.1.call-start = ((), (), s32[]{:S(2)}) async-start(), calls=%async_computation.3 | async-start | bytes 1081344 | tf_op jit(solution)/shard_map/reduce_scatter | solution.py:213
  644.0 250.0 %reduce-scatter.3.cloned.1.call-start = ((), (), s32[]{:S(2)}) async-start(), calls=%async_computation.2 | async-start | bytes 1081344 | tf_op jit(solution)/shard_map/reduce_scatter | solution.py:210
  646.8 363.3 %all-reduce.5.cloned.1.call-start = ((), (), s32[]{:S(2)}) async-start(), calls=%async_computation.5 | async-start | bytes 8388608 | tf_op jit(solution)/shard_map/psum | solution.py:222
  648.6 89.4 %collective-permute-start.3 = (bf16[512,1024]{1,0:T(8,128)(2,1)S(1)}, bf16[512,1024]{1,0:T(8,128)(2,1)S(1)}, u32[]{:S(2)}, u32[]{:S(2)}) collective-permute-start(bf16[512,1024]{1,0:T(8,128)(2,1)S(1)} %slice.88), channel_id=1, source_target_pairs={{1,0},{2,1},{3,2},{4,3},{5,4},{6,5},{7,6},{8,7},{9,8},{10,9},{11,1... | collective-permute-start | bytes 3145736 | tf_op jit(solution)/shard_map/ppermute | solution.py:15
  733.4 18.1 %copy-start.2 = (f32[1024,1024]{1,0:T(8,128)S(1)}, f32[1024,1024]{1,0:T(8,128)}, u32[]{:S(2)}) copy-start(f32[1024,1024]{1,0:T(8,128)} %get-tuple-element.279) | copy-start | bytes 12582916
  735.3 16.1 %collective-permute-start.2 = (bf16[512,1024]{1,0:T(8,128)(2,1)S(1)}, bf16[512,1024]{1,0:T(8,128)(2,1)S(1)}, u32[]{:S(2)}, u32[]{:S(2)}) collective-permute-start(bf16[512,1024]{1,0:T(8,128)(2,1)S(1)} %slice.89), channel_id=1, source_target_pairs={{1,0},{2,1},{3,2},{4,3},{5,4},{6,5},{7,6},{8,7},{9,8},{10,9},{11,1... | collective-permute-start | bytes 3145736 | tf_op jit(solution)/shard_map/ppermute | solution.py:15
  898.9 116.2 %copy-start.1 = (bf16[1024,1024]{1,0:T(8,128)(2,1)S(1)}, bf16[1024,1024]{1,0:T(8,128)(2,1)}, u32[]{:S(2)}) copy-start(bf16[1024,1024]{1,0:T(8,128)(2,1)} %param.22) | copy-start | bytes 6291460
Sparse Core Ops, SparseCore 0:
  11.4 52.4 all-gather.6
  66.7 41.9 all-gather.4
  641.3 92.0 all-reduce.2
  737.7 75.4 reduce-scatter.4
  817.2 76.7 reduce-scatter.2
  897.5 112.4 all-reduce.4
